TPU v7x, 256 devices: a whole 4x4x8 slice. The times are simulated.
256 devices in a mesh: rows: 8 (over z_hi, core), pairs: 32 (over y, z_lo, x).
Axes of the slice: x: 4, y: 4, z: 8 (z_hi: 4, z_lo: 2; z = z_hi * 2 + z_lo), core: 2. Of those that a mesh axis runs over, the one named last changes fastest.
Arguments:
- snapshot: float32 [16384, 16384], P('rows', 'pairs'), may hold values from -60 to 60, as said below
- plan: int32 [3, 32], P(None, 'pairs'), may hold values from 0 to 1
Outputs:
- rotated_matrix: float32 [16384, 16384], P('rows', 'pairs')
Inputs may be any that keep to these rules, and one draw needn't show every extreme that they name: `plan`: 1 says that the second held block moves on, 0 the first. `snapshot`: columns have scales of 1 to 10.
All inputs are finite; a program needn't handle non-finite values.
Results may differ from a plain program's by a relative error of at most 0.00012.
Values sent between devices are 32-bit elements; how exact they have to be, the bound alone decides.
A program may use at most 64 MiB of HBM per device.

v0:
```python
import jax
import jax.numpy as jnp
from jax import lax
from jax.sharding import PartitionSpec as P

STEPS = 3


epsilon = 1e-06


def shifted(block, axis, distance):
    devices = range(lax.axis_size(axis))
    route = [((i - distance) % len(devices), i) for i in devices]
    return lax.ppermute(block, axis, route)


def polar_factor(cross, left_sq, right_sq):
    width = cross.shape[0]
    scaled = (
        0.5 * cross * lax.rsqrt(left_sq + epsilon)[:, None] * lax.rsqrt(right_sq + epsilon)[None, :]
    )
    scaled = scaled / (1.0 + jnp.sqrt(jnp.sum(scaled * scaled)))
    zeros = jnp.zeros((width, width), jnp.float32)
    upper = jnp.concatenate([zeros, scaled], axis=1)
    lower = jnp.concatenate([-scaled.T, zeros], axis=1)
    rotation = (
        jnp.eye(2 * width, dtype=jnp.float32) + jnp.concatenate([upper, lower], axis=0)
    ) / jnp.sqrt(jnp.float32(1.25))
    for sweep_iter in range(2):
        product = jnp.dot(rotation.T, rotation, precision=lax.Precision.HIGHEST)
        rotation = 1.5 * rotation - 0.5 * jnp.dot(
            rotation, product, precision=lax.Precision.HIGHEST
        )
    return rotation


def inner_cols(first, second):
    return lax.dot_general(first, second, (((0,), (0,)), ((), ())), precision=lax.Precision.HIGHEST)


def pass_on(moving):
    return shifted(moving, "pairs", 1)


def body(snapshot, plan):
    width = snapshot.shape[1] // 2
    current = snapshot
    for sweep_step in range(STEPS):
        gram = lax.psum(inner_cols(current, current), "rows")
        cross = gram[:width, width:]
        diagonal = jnp.diagonal(gram)
        left_sq = diagonal[:width]
        right_sq = diagonal[width:]
        rotation = polar_factor(cross, left_sq, right_sq)
        chosen = plan[sweep_step, 0] == 1
        rotated = jnp.dot(current, rotation, precision=lax.Precision.HIGHEST)
        moving = jnp.where(chosen, rotated[:, width:], rotated[:, :width])
        staying = jnp.where(chosen, rotated[:, :width], rotated[:, width:])
        arrived = pass_on(moving)
        current = jnp.concatenate([staying, arrived], axis=1)
    return current


def solution(mesh):
    placed = (P("rows", "pairs"), P(None, "pairs"))
    return jax.shard_map(
        body, mesh=mesh, in_specs=placed, out_specs=P("rows", "pairs"), check_vma=False
    )
```

profile of v0, /device:TPU:5, one launch (start us, length us, event | category | flops | bytes accessed | tf_op | source)
XLA Modules:
  0.0 505.4 jit_solution(4973023717119641516)
XLA Ops:
  6.5 0.0 copy-start.5
  6.5 0.0 all-reduce.10.cloned.1.call-start
  6.5 11.1 %fusion.75 = f32[512,512]{1,0:T(8,128)} fusion(f32[2048,512]{1,0:T(8,128)} %param.2), kind=kOutput, calls=%fused_computation.116 | convolution fusion | flops 6442450944 | bytes 5242880 | tf_op jit(solution)/shard_map/dot_general | solution.py:39
  17.6 0.0 all-reduce.10.cloned.1.call-update
  17.7 0.0 all-reduce.12.cloned.1.call-start
  17.7 0.0 copy-done.5
  17.7 0.7 fusion.74
  19.0 77.4 %all-reduce.10.cloned.1.call-done = f32[512,512]{1,0:T(8,128)} async-done(((f32[512,512]{1,0:T(8,128)}), f32[512,512]{1,0:T(8,128)}) %all-reduce.10.cloned.1.call-update) | async-done | bytes 1048592 | tf_op jit(solution)/shard_map/psum | solution.py:50
  96.4 9.0 %gather_fusion = f32[512]{0:T(512)S(1)} fusion(f32[512,512]{1,0:T(8,128)} %all-reduce.10.cloned.1.call-done, s32[512]{0:T(512)S(1)} %bitcast.33), kind=kCustom, calls=%fused_computation | custom fusion | bytes 8192 | tf_op jit(solution)/shard_map/jit(diagonal)/cond/branch_0_fun/gather | solution.py:52
  105.4 1.7 multiply_reduce_fusion.2
  107.8 1.1 negate_bitcast_fusion.2
  108.9 0.1 copy.10
  109.0 1.8 fusion.17
  110.9 1.9 fusion.9
  112.8 0.0 copy-start
  112.8 1.9 fusion.76
  114.7 1.9 fusion.8
  116.7 0.0 copy-done
  116.7 7.7 %convolution_bitcast_fusion = f32[2048,512]{0,1:T(8,128)S(1)} fusion(f32[512,512]{0,1:T(8,128)S(1)} %fusion.8, f32[2048,512]{1,0:T(8,128)S(1)} %copy-done), kind=kOutput, calls=%fused_computation.10 | convolution fusion | flops 6442450944 | bytes 9437184 | tf_op jit(solution)/shard_map/dot_general | solution.py:57
  124.4 0.6 slice_select_fusion.5
  124.9 1.0 collective-permute-start
  125.9 44.4 %collective-permute-done = f32[2048,256]{0,1:T(8,128)S(1)} collective-permute-done((f32[2048,256]{0,1:T(8,128)S(1)}, f32[2048,256]{0,1:T(8,128)S(1)}, u32[]{:S(2)}, u32[]{:S(2)}) %collective-permute-start) | collective-permute-done | bytes 2097184 | tf_op jit(solution)/shard_map/ppermute | solution.py:15
  170.3 0.0 copy-start.3
  170.3 1.3 copy-done.3
  171.6 7.9 %fusion.3 = f32[512,512]{1,0:T(8,128)} fusion(f32[2048,256]{0,1:T(8,128)S(1)} %collective-permute-done, f32[2048,256]{0,1:T(8,128)S(1)} %get-tuple-element.15), kind=kOutput, calls=%fused_computation.9 | convolution fusion | flops 6443499520 | bytes 5242880 | tf_op jit(solution)/shard_map/dot_general | solution.py:39
  179.5 0.0 all-reduce.12.cloned.1.call-update
  179.6 0.0 all-reduce.14.cloned.1.call-start
  180.3 76.3 %all-reduce.12.cloned.1.call-done = f32[512,512]{1,0:T(8,128)} async-done(((f32[512,512]{1,0:T(8,128)}), f32[512,512]{1,0:T(8,128)}) %all-reduce.12.cloned.1.call-update) | async-done | bytes 1048592 | tf_op jit(solution)/shard_map/psum | solution.py:50
  256.6 8.9 %gather_fusion.1 = f32[512]{0:T(512)S(1)} fusion(f32[512,512]{1,0:T(8,128)} %all-reduce.12.cloned.1.call-done, s32[512]{0:T(512)S(1)} %bitcast.34), kind=kCustom, calls=%fused_computation.1 | custom fusion | bytes 8192 | tf_op jit(solution)/shard_map/jit(diagonal)/cond/branch_0_fun/gather | solution.py:52
  265.6 1.8 multiply_reduce_fusion.1
  268.0 1.1 negate_bitcast_fusion.1
  269.1 0.1 copy.20
  269.2 1.8 fusion.14
  271.1 1.9 fusion.7
  273.0 0.0 copy-start.4
  273.0 1.9 fusion.77
  274.9 2.0 fusion.6
  276.9 0.0 copy-done.4
  276.9 7.8 %fusion.2 = f32[2048,512]{0,1:T(8,128)S(1)} fusion(f32[512,512]{0,1:T(8,128)S(1)} %fusion.6, f32[2048,256]{0,1:T(8,128)S(1)} %copy-done.4, f32[2048,256]{0,1:T(8,128)S(1)} %get-tuple-element.15), kind=kOutput, calls=%fused_computation.8 | convolution fusion | flops 6443499520 | bytes 9437184 | tf_op jit(solution)/shard_map/dot_general | solution.py:57
  284.7 0.6 slice_select_fusion.3
  285.3 1.0 collective-permute-start.1
  286.3 44.4 %collective-permute-done.1 = f32[2048,256]{0,1:T(8,128)S(1)} collective-permute-done((f32[2048,256]{0,1:T(8,128)S(1)}, f32[2048,256]{0,1:T(8,128)S(1)}, u32[]{:S(2)}, u32[]{:S(2)}) %collective-permute-start.1) | collective-permute-done | bytes 2097184 | tf_op jit(solution)/shard_map/ppermute | solution.py:15
  330.7 0.0 copy-start.1
  330.7 1.3 copy-done.1
  332.0 7.9 %fusion.1 = f32[512,512]{1,0:T(8,128)} fusion(f32[2048,256]{0,1:T(8,128)S(1)} %collective-permute-done.1, f32[2048,256]{0,1:T(8,128)S(1)} %get-tuple-element.13), kind=kOutput, calls=%fused_computation.7 | convolution fusion | flops 6443499520 | bytes 5242880 | tf_op jit(solution)/shard_map/dot_general | solution.py:39
  339.9 0.0 all-reduce.14.cloned.1.call-update
  340.6 76.4 %all-reduce.14.cloned.1.call-done = f32[512,512]{1,0:T(8,128)} async-done(((f32[512,512]{1,0:T(8,128)}), f32[512,512]{1,0:T(8,128)}) %all-reduce.14.cloned.1.call-update) | async-done | bytes 1048592 | tf_op jit(solution)/shard_map/psum | solution.py:50
  417.0 9.2 %gather_fusion.2 = f32[512]{0:T(512)S(1)} fusion(f32[512,512]{1,0:T(8,128)} %all-reduce.14.cloned.1.call-done, s32[512]{0:T(512)S(1)} %bitcast.35), kind=kCustom, calls=%fused_computation.2 | custom fusion | bytes 8192 | tf_op jit(solution)/shard_map/jit(diagonal)/cond/branch_0_fun/gather | solution.py:52
  426.2 1.7 multiply_reduce_fusion
  428.6 1.1 negate_bitcast_fusion
  429.6 0.1 copy.21
  429.8 1.8 fusion.11
  431.6 1.9 fusion.5
  433.5 0.0 copy-start.2
  433.5 1.9 fusion.78
  435.4 2.0 fusion.4
  437.4 0.0 copy-done.2
  437.4 7.8 %fusion = f32[2048,512]{0,1:T(8,128)S(1)} fusion(f32[512,512]{0,1:T(8,128)S(1)} %fusion.4, f32[2048,256]{0,1:T(8,128)S(1)} %copy-done.2, f32[2048,256]{0,1:T(8,128)S(1)} %get-tuple-element.13), kind=kOutput, calls=%fused_computation.6 | convolution fusion | flops 6443499520 | bytes 9437184 | tf_op jit(solution)/shard_map/dot_general | solution.py:57
  445.2 0.3 slice_select_fusion.1
  445.5 1.0 collective-permute-start.2
  446.5 44.4 %collective-permute-done.2 = f32[2048,256]{0,1:T(8,128)S(1)} collective-permute-done((f32[2048,256]{0,1:T(8,128)S(1)}, f32[2048,256]{0,1:T(8,128)S(1)}, u32[]{:S(2)}, u32[]{:S(2)}) %collective-permute-start.2) | collective-permute-done | bytes 2097184 | tf_op jit(solution)/shard_map/ppermute | solution.py:15
  490.9 2.4 pad_maximum_fusion.2
  493.3 5.3 %copy.16 = f32[2048,512]{1,0:T(8,128)} copy(f32[2048,512]{0,1:T(8,128)} %pad_maximum_fusion.2) | data formatting | bytes 8388608 | tf_op jit(solution)/shard_map/concatenate | solution.py:61
  (4 shorter events, 0.0 us)
Async XLA Ops:
  6.5 11.2 %copy-start.5 = (s32[3,1]{0,1:T(1,128)S(1)}, s32[3,1]{0,1:T(1,128)}, u32[]{:S(2)}) copy-start(s32[3,1]{0,1:T(1,128)} %param.3) | copy-start | bytes 40
  6.5 89.8 %all-reduce.10.cloned.1.call-start = ((), (), s32[]{:S(2)}) async-start(), calls=%async_computation | async-start | bytes 2097152 | tf_op jit(solution)/shard_map/psum | solution.py:50
  17.7 239.0 %all-reduce.12.cloned.1.call-start = ((), (), s32[]{:S(2)}) async-start(), calls=%async_computation.1 | async-start | bytes 2097152 | tf_op jit(solution)/shard_map/psum | solution.py:50
  112.8 3.8 copy-start
  124.9 45.3 %collective-permute-start = (f32[2048,256]{0,1:T(8,128)S(1)}, f32[2048,256]{0,1:T(8,128)S(1)}, u32[]{:S(2)}, u32[]{:S(2)}) collective-permute-start(f32[2048,256]{0,1:T(8,128)S(1)} %get-tuple-element.16), channel_id=1, source_target_pairs={{31,0},{0,1},{1,2},{2,3},{3,4},{4,5},{5,6},{6,7},{7,8},{8,9},{9,10... | collective-permute-start | bytes 6291464 | tf_op jit(solution)/shard_map/ppermute | solution.py:15
  170.3 1.3 copy-start.3
  179.6 237.4 %all-reduce.14.cloned.1.call-start = ((), (), s32[]{:S(2)}) async-start(), calls=%async_computation.2 | async-start | bytes 2097152 | tf_op jit(solution)/shard_map/psum | solution.py:50
  273.0 3.9 copy-start.4
  285.3 45.3 %collective-permute-start.1 = (f32[2048,256]{0,1:T(8,128)S(1)}, f32[2048,256]{0,1:T(8,128)S(1)}, u32[]{:S(2)}, u32[]{:S(2)}) collective-permute-start(f32[2048,256]{0,1:T(8,128)S(1)} %get-tuple-element.14), channel_id=1, source_target_pairs={{31,0},{0,1},{1,2},{2,3},{3,4},{4,5},{5,6},{6,7},{7,8},{8,9},{9,10... | collective-permute-start | bytes 6291464 | tf_op jit(solution)/shard_map/ppermute | solution.py:15
  330.7 1.3 copy-start.1
  433.5 3.9 copy-start.2
  445.5 45.3 %collective-permute-start.2 = (f32[2048,256]{0,1:T(8,128)S(1)}, f32[2048,256]{0,1:T(8,128)S(1)}, u32[]{:S(2)}, u32[]{:S(2)}) collective-permute-start(f32[2048,256]{0,1:T(8,128)S(1)} %get-tuple-element.12), channel_id=1, source_target_pairs={{31,0},{0,1},{1,2},{2,3},{3,4},{4,5},{5,6},{6,7},{7,8},{8,9},{9,10... | collective-permute-start | bytes 6291464 | tf_op jit(solution)/shard_map/ppermute | solution.py:15
Sparse Core Ops, SparseCore 0:
  17.8 78.5 all-reduce.9
  179.7 76.8 all-reduce.11
  340.0 76.8 all-reduce.13
where the time goes:
time: 515 us; the launch traced here: 505 us
  waiting for transfers between devices  363 us (70%)
  matrix products  73 us (14%)
  local copies, waits for them, and re-layouts  36.1 us (7%)
  between operations  17.7 us (3%)
  other arithmetic  12.3 us (2%)
    psum x3, waiting for transfers between devices, body(): gram = lax.psum(inner_cols(current, current), 'rows')  230 us
    ppermute x3, waiting for transfers between devices, shifted(): return lax.ppermute(block, axis, route)  133 us
    gather x3, local copies, waits for them, and re-layouts, body(): diagonal = jnp.diagonal(gram)  27.1 us
    dot_general x3, matrix products, inner_cols(): lax.dot_general(first, second, (((0,), (0,)), ((), ())), precision=lax.Pr...  26.9 us
    dot_general x3, matrix products, body(): rotated = jnp.dot(current, rotation, precision=lax.Precision.HIGHEST)  23.3 us
    dot_general x6, matrix products, polar_factor(): jnp.dot(rotation, product, precision=lax.Precision.HIGHEST)  11.7 us
    dot_general x6, matrix products, polar_factor(): product = jnp.dot(rotation.T, rotation, precision=lax.Precision.HIGHEST)  11.1 us
  transfers between devices with their start and end apart: 6, of which 6 were waited for; matrix products, arithmetic and copies ran while one was open for 0% of the time, Pallas kernels for 0%

commit v1 on v0

v1 whole, which is shorter than its diff:
```python
import functools

import jax
import jax.numpy as jnp
from jax import lax
from jax.experimental import pallas as pl
from jax.experimental.pallas import tpu as pltpu
from jax.sharding import PartitionSpec as P
from numpy.polynomial import Polynomial

STEPS = 3
CHUNKS = 8
EPSILON = 1e-06
MESH = pl.DeviceIdType.MESH


def gains():
    product = Polynomial([0.8, 0.8])
    first = 1.5 - 0.5 * product
    second = 1.5 - 0.5 * product * first * first
    return [float(c) for c in (first * second / 1.25**0.5).coef]


def split(x):
    high = x.astype(jnp.bfloat16)
    return high, (x - high.astype(jnp.float32)).astype(jnp.bfloat16)


def dot(a, b, dims=(1, 0)):
    def one(x, y):
        return lax.dot_general(
            x, y, (((dims[0],), (dims[1],)), ((), ())), preferred_element_type=jnp.float32
        )

    return one(a[0], b[0]) + (one(a[0], b[1]) + one(a[1], b[0]))


def polynomial(square, eye, g):
    s = split(square)
    square2 = dot(s, s)
    return (g[0] * eye + g[1] * square + g[2] * square2) + dot(
        split(square2), split(g[3] * square + g[4] * square2)
    )


def kernel(
    n_pairs,
    snapshot,
    plan,
    out,
    data,
    staged,
    parted,
    partner_part,
    shares,
    arrived,
    cross,
    weights_high,
    weights_low,
    load_sem,
    pair_sem,
    share_sem,
    gather_sem,
    pass_sem,
    block_sem,
    last_sem,
):
    rows, width = snapshot.shape[0], snapshot.shape[1] // 2
    chunk, half, quarter = rows // CHUNKS, width // 2, width // 8
    r, p = lax.axis_index("rows"), lax.axis_index("pairs")
    core, z = lax.rem(r, 2), lax.div(r, 2)
    g = gains()

    def pair_at(distance):
        return lax.rem(p + distance + 2 * n_pairs, n_pairs)

    def chunk_rows(c):
        return pl.ds(pl.multiple_of(c * chunk, chunk), chunk)

    def row_at(c, z_index):
        return pl.ds(pl.multiple_of(c * half + z_index * quarter, quarter), quarter)

    def load(c, side):
        return pltpu.make_async_copy(
            snapshot.at[chunk_rows(c), pl.ds(side * width, width)],
            data.at[0, side, chunk_rows(c)],
            load_sem.at[c, side],
        )

    for c in range(CHUNKS):
        for side in range(2):
            load(c, side).start()

    barrier = pltpu.get_barrier_semaphore()
    peers = [(lax.rem(z + j, 4) * 2 + core, p) for j in (1, 2, 3)]
    peers += [(r, pair_at(d)) for d in (1, -1, 2, -2, 3, -3)]
    peers += [(z * 2 + 1 - core, pair_at(d)) for d in (0, 1, -1, 2, -2)]
    for peer in peers:
        pl.semaphore_signal(barrier, inc=1, device_id=peer, device_id_type=MESH)

    def remote(src, dst, sems, device):
        return pltpu.make_async_remote_copy(
            src_ref=src,
            dst_ref=dst,
            send_sem=sems.at[0],
            recv_sem=sems.at[1],
            device_id=device,
            device_id_type=MESH,
        )

    eye = (
        lax.broadcasted_iota(jnp.int32, (width, width), 0)
        == lax.broadcasted_iota(jnp.int32, (width, width), 1)
    ).astype(jnp.float32)

    def sent(step, c):
        return remote(
            staged.at[0, chunk_rows(c)],
            data.at[step + 1, 1 - core, chunk_rows(c)],
            block_sem.at[step, c],
            (r, pair_at(1 - 2 * core)),
        )

    def last_first(c):
        return remote(
            staged.at[0, chunk_rows(c)],
            out.at[chunk_rows(c), pl.ds(pl.multiple_of((1 - core) * width, width), width)],
            block_sem.at[STEPS - 1, c],
            (r, pair_at(1 + core)),
        )

    def last_second(c):
        return remote(
            staged.at[1, chunk_rows(c)],
            out.at[chunk_rows(c), pl.ds(width, width)],
            last_sem.at[c],
            (r, pair_at(3)),
        )

    def last_local(c):
        return pltpu.make_async_copy(
            staged.at[1, chunk_rows(c)],
            out.at[chunk_rows(c), pl.ds(0, width)],
            last_sem.at[c, 0],
        )

    for step in range(STEPS):
        parted[step] = jnp.zeros(parted.shape[1:], jnp.float32)

        @pl.loop(0, CHUNKS)
        def _(c):
            if step == 0:
                load(c, 0).wait()
                load(c, 1).wait()
            else:
                sent(step - 1, c).wait_recv()
            left = data[step, 0, chunk_rows(c)]
            right = data[step, 1, chunk_rows(c)]
            product = dot(split(left), split(right), (0, 0))
            parted[step, 0, :half] += product[:half]
            parted[step, 1, :half] += product[half:]
            parted[step, 0, half : half + 1] += jnp.sum(left * left, axis=0, keepdims=True)
            parted[step, 0, half + 1 : half + 2] += jnp.sum(right * right, axis=0, keepdims=True)

        choice = plan[step, 0].astype(jnp.float32) * (1 - core).astype(jnp.float32)
        parted[step, 0, half + 2 : half + 3] = jnp.full((1, width), 1.0, jnp.float32) * choice
        parted[step, 1, half:] = parted[step, 0, half:]

        if step == 0:
            pl.semaphore_wait(barrier, len(peers))

        partner = (z * 2 + 1 - core, pair_at(step * (2 * core - 1)))
        exchange = remote(
            parted.at[step, 1 - core], partner_part.at[step], pair_sem.at[step], partner
        )
        exchange.start()
        exchange.wait_recv()
        for k in range(4):
            at = slice(k * quarter, (k + 1) * quarter)
            shares[step, k, :quarter] = parted[step, core, at] + partner_part[step, at]
            shares[step, k, quarter:] = parted[step, core, half:] + partner_part[step, half:]

        def share(j):
            k = lax.rem(z + j, 4)
            return remote(
                shares.at[step, k], arrived.at[step, z], share_sem.at[step, j], (k * 2 + core, p)
            )

        def share_in(j):
            return remote(
                shares.at[step, z],
                arrived.at[step, lax.rem(z + 4 - j, 4)],
                share_sem.at[step, j],
                (r, pair_at(1)),
            )

        for j in (2, 1, 3):
            share(j).start()
        arrived[step, z] = shares[step, z]
        for j in (1, 3, 2):
            share_in(j).wait_recv()
        total = (arrived[step, 0] + arrived[step, 1]) + (arrived[step, 2] + arrived[step, 3])
        mine = row_at(core, z)
        cross[step, mine] = total[:quarter]

        def gather(j):
            return remote(
                cross.at[step, mine],
                cross.at[step, mine],
                gather_sem.at[step, j],
                (lax.rem(z + j, 4) * 2 + core, p),
            )

        def gather_in(j):
            at = row_at(core, lax.rem(z + 4 - j, 4))
            return remote(
                cross.at[step, at], cross.at[step, at], gather_sem.at[step, j], (r, pair_at(1))
            )

        def passed(j):
            at = row_at(core, lax.rem(z + 4 - j, 4))
            return remote(cross.at[step, at], cross.at[step, at], pass_sem.at[step, j], partner)

        def passed_in(j):
            at = row_at(1 - core, lax.rem(z + 4 - j, 4))
            return remote(cross.at[step, at], cross.at[step, at], pass_sem.at[step, j], partner)

        for j in (2, 1, 3):
            gather(j).start()
        passed(0).start()
        for j in (1, 3, 2):
            gather_in(j).wait_recv()
            passed(j).start()

        squares = total[quarter:]
        left_scale = lax.rsqrt(squares[0:1] + EPSILON)
        right_scale = lax.rsqrt(squares[1:2] + EPSILON)
        left_scale = jnp.broadcast_to(left_scale, (width, width)).T
        for j in range(4):
            passed_in(j).wait_recv()

        scaled = 0.5 * cross[step] * left_scale * right_scale
        scaled = scaled / (1.0 + jnp.sqrt(jnp.sum(scaled * scaled)))
        e = split(scaled)
        upper = polynomial(dot(e, e, (1, 1)), eye, g)
        lower = polynomial(dot(e, e, (0, 0)), eye, g)
        mixed = dot(split(upper), e)
        turned = -mixed.T
        chosen = squares[2:3] * 0.25
        flip = core.astype(jnp.float32)
        second_sent = (chosen * (1.0 - flip) + (1.0 - chosen) * flip) > 0.5
        for at, zero, one in (
            (slice(0, width), upper, mixed),
            (slice(width, 2 * width), turned, lower),
        ):
            kept_high, kept_low = split(jnp.where(second_sent, zero, one))
            sent_high, sent_low = split(jnp.where(second_sent, one, zero))
            weights_high[at, :width] = kept_high
            weights_high[at, width:] = sent_high
            weights_low[at, :width] = kept_low
            weights_low[at, width:] = sent_low

        if step > 0:

            @pl.loop(0, CHUNKS)
            def _(c):
                sent(step - 1, c).wait_send()

        @pl.loop(0, CHUNKS)
        def _(c):
            at = chunk_rows(c)
            high, low = split(jnp.concatenate([data[step, 0, at], data[step, 1, at]], axis=1))
            result = dot((high, low), (weights_high[...], weights_low[...]))
            staged[0, at] = result[:, width:]
            if step < STEPS - 1:
                sent(step, c).start()
                data[step + 1, core, at] = result[:, :width]
            else:
                last_first(c).start()
                staged[1, at] = result[:, :width]

                @pl.when(core == 0)
                def _():
                    last_local(c).start()

                @pl.when(core == 1)
                def _():
                    last_second(c).start()

        exchange.wait_send()
        for j in (1, 2, 3):
            share(j).wait_send()
            gather(j).wait_send()
        for j in range(4):
            passed(j).wait_send()

    @pl.loop(0, CHUNKS)
    def _(c):
        last_first(c).wait()

        @pl.when(core == 0)
        def _():
            last_local(c).wait()

        @pl.when(core == 1)
        def _():
            last_second(c).wait()


def body(snapshot, plan):
    rows, width = snapshot.shape[0], snapshot.shape[1] // 2
    half, quarter = width // 2, width // 8
    dma = pltpu.SemaphoreType.DMA
    f32 = jnp.float32
    return pl.pallas_call(
        functools.partial(kernel, lax.axis_size("pairs")),
        out_shape=jax.ShapeDtypeStruct(snapshot.shape, f32),
        in_specs=[
            pl.BlockSpec(memory_space=pl.ANY),
            pl.BlockSpec(memory_space=pltpu.SMEM),
        ],
        out_specs=pl.BlockSpec(memory_space=pl.ANY),
        scratch_shapes=[
            pltpu.VMEM((STEPS, 2, rows, width), f32),
            pltpu.VMEM((2, rows, width), f32),
            pltpu.VMEM((STEPS, 2, half + 8, width), f32),
            pltpu.VMEM((STEPS, half + 8, width), f32),
            pltpu.VMEM((STEPS, 4, quarter + 8, width), f32),
            pltpu.VMEM((STEPS, 4, quarter + 8, width), f32),
            pltpu.VMEM((STEPS, width, width), f32),
            pltpu.VMEM((2 * width, 2 * width), jnp.bfloat16),
            pltpu.VMEM((2 * width, 2 * width), jnp.bfloat16),
            dma((CHUNKS, 2)),
            dma((STEPS, 2)),
            dma((STEPS, 4, 2)),
            dma((STEPS, 4, 2)),
            dma((STEPS, 4, 2)),
            dma((STEPS, CHUNKS, 2)),
            dma((CHUNKS, 2)),
        ],
        compiler_params=pltpu.CompilerParams(
            collective_id=0, has_side_effects=True, vmem_limit_bytes=44 * 1024 * 1024
        ),
    )(snapshot, plan)


def solution(mesh):
    placed = (P("rows", "pairs"), P(None, "pairs"))
    return jax.shard_map(
        body, mesh=mesh, in_specs=placed, out_specs=P("rows", "pairs"), check_vma=False
    )
```

time: 515 us -> 219 us (0.43); the launches traced: 505 us -> 219 us
  waiting for transfers between devices: 363 us -> 0 us
  Pallas kernels: 0 us -> 214 us
  matrix products: 73 us -> 0 us
  local copies, waits for them, and re-layouts: 36.1 us -> 4.94 us
  between operations: 17.7 us -> 0.01 us
  other arithmetic: 12.3 us -> 0 us
    psum x3 -> x0, waiting for transfers between devices: 230 us -> none  [body(): gram = lax.psum(inner_cols(current, current), 'rows')]
    pallas_call x0 -> x1, Pallas kernels: none -> 214 us  [body(): pl.pallas_call(functools.partial(kernel, lax.axis_size('pairs')), out_sha...]
    ppermute x3 -> x0, waiting for transfers between devices: 133 us -> none  [shifted(): return lax.ppermute(block, axis, route)]
    dot_general x18 -> x0, matrix products: 73 us -> none  [the longest x3 26.9 us: inner_cols(): lax.dot_general(first, second, (((0,), (0,)), ((), ())), precision=lax.Pr...]
    gather x3 -> x0, local copies, waits for them, and re-layouts: 27.1 us -> none  [body(): diagonal = jnp.diagonal(gram)]
    concatenate x1 -> x0, local copies, waits for them, and re-layouts: 5.34 us -> none  [body(): current = jnp.concatenate([staying, arrived], axis=1)]
    reduce_sum x3 -> x0, other arithmetic: 5.18 us -> none  [polar_factor(): scaled = scaled / (1.0 + jnp.sqrt(jnp.sum(scaled * scaled)))]
  transfers between devices with their start and end apart: 6 -> 0, of which waited for: 6 -> 0; matrix products, arithmetic and copies ran while one was open for 0% -> 0% of each run, Pallas kernels for 0% -> 0%
where the time goes in v1:
time: 219 us
  Pallas kernels  214 us (98%)
  local copies, waits for them, and re-layouts  4.94 us (2%)
    pallas_call x1, Pallas kernels, body(): pl.pallas_call(functools.partial(kernel, lax.axis_size('pairs')), out_sha...  214 us
    unnamed x4, local copies, waits for them, and re-layouts  4.94 us

profile of v1, /device:TPU:5, one launch (start us, length us, event | category | flops | bytes accessed | tf_op | source)
XLA Modules:
  0.0 219.2 jit_solution(5413025295660708302)
XLA Ops:
  0.0 0.7 copy.3.plan
  0.7 0.0 copy-start
  0.7 2.2 copy-done
  2.9 214.3 %shard_map.28 = f32[2048,512]{1,0:T(8,128)S(1)} custom-call(f32[2048,512]{1,0:T(8,128)S(1)} %copy-done, s32[3,1]{1,0:T(4,128)S(1)} %copy.3.plan), custom_call_target="tpu_custom_call" | custom-call | tf_op jit(solution)/shard_map/pallas_call | solution.py:315
  217.2 2.0 copy.5
Async XLA Ops:
  0.7 2.2 copy-start

commit v2 on v1

--- a/solution.py
+++ b/solution.py
@@ -10,6 +10,7 @@
 
 STEPS = 3
 CHUNKS = 8
+LINE = 4
 EPSILON = 1e-06
 MESH = pl.DeviceIdType.MESH
 
@@ -50,6 +51,8 @@
     out,
     data,
     staged,
+    relayed,
+    squares,
     parted,
     partner_part,
     shares,
@@ -58,17 +61,20 @@
     weights_high,
     weights_low,
     load_sem,
+    square_sem,
     pair_sem,
     share_sem,
     gather_sem,
     pass_sem,
     block_sem,
-    last_sem,
+    staying_sem,
+    moving_sem,
+    relay_sem,
 ):
     rows, width = snapshot.shape[0], snapshot.shape[1] // 2
     chunk, half, quarter = rows // CHUNKS, width // 2, width // 8
     r, p = lax.axis_index("rows"), lax.axis_index("pairs")
-    core, z = lax.rem(r, 2), lax.div(r, 2)
+    core, z, x = lax.rem(r, 2), lax.div(r, 2), lax.rem(p, LINE)
     g = gains()
 
     def pair_at(distance):
@@ -93,8 +99,12 @@
 
     barrier = pltpu.get_barrier_semaphore()
     peers = [(lax.rem(z + j, 4) * 2 + core, p) for j in (1, 2, 3)]
-    peers += [(r, pair_at(d)) for d in (1, -1, 2, -2, 3, -3)]
-    peers += [(z * 2 + 1 - core, pair_at(d)) for d in (0, 1, -1, 2, -2)]
+    peers += [(r, pair_at(d)) for d in (1, -1, 2, -2, 3, -3, 4, -4)]
+    peers += [
+        (lax.rem(z + j, 4) * 2 + 1 - core, pair_at(step * (2 * core - 1)))
+        for j in range(4)
+        for step in range(STEPS)
+    ]
     for peer in peers:
         pl.semaphore_signal(barrier, inc=1, device_id=peer, device_id_type=MESH)
 
@@ -121,31 +131,55 @@
             (r, pair_at(1 - 2 * core)),
         )
 
-    def last_first(c):
+    first_half, second_half = pl.ds(0, width), pl.ds(width, width)
+    detours = jnp.where(core == 0, x == LINE - 1, x != 0)
+    relays = jnp.where(core == 0, x == 0, x != 0)
+
+    def staying_local(c):
+        return pltpu.make_async_copy(
+            staged.at[0, chunk_rows(c)], out.at[chunk_rows(c), first_half], staying_sem.at[c, 0]
+        )
+
+    def staying_back(c):
         return remote(
             staged.at[0, chunk_rows(c)],
-            out.at[chunk_rows(c), pl.ds(pl.multiple_of((1 - core) * width, width), width)],
-            block_sem.at[STEPS - 1, c],
-            (r, pair_at(1 + core)),
-        )
-
-    def last_second(c):
+            out.at[chunk_rows(c), first_half],
+            staying_sem.at[c],
+            (r, pair_at(2)),
+        )
+
+    def moving_direct(c):
         return remote(
             staged.at[1, chunk_rows(c)],
-            out.at[chunk_rows(c), pl.ds(width, width)],
-            last_sem.at[c],
-            (r, pair_at(3)),
-        )
-
-    def last_local(c):
-        return pltpu.make_async_copy(
-            staged.at[1, chunk_rows(c)],
-            out.at[chunk_rows(c), pl.ds(0, width)],
-            last_sem.at[c, 0],
+            out.at[chunk_rows(c), second_half],
+            moving_sem.at[c],
+            (r, pair_at(1 + 2 * core)),
+        )
+
+    def moving_detour(c):
+        return pltpu.make_async_remote_copy(
+            src_ref=staged.at[1, chunk_rows(c)],
+            dst_ref=relayed.at[chunk_rows(c)],
+            send_sem=moving_sem.at[c, 0],
+            recv_sem=relay_sem.at[c, 1],
+            device_id=(r, pair_at(7 * core - 3)),
+            device_id_type=MESH,
+        )
+
+    def relay(c):
+        return pltpu.make_async_remote_copy(
+            src_ref=relayed.at[chunk_rows(c)],
+            dst_ref=out.at[chunk_rows(c), second_half],
+            send_sem=relay_sem.at[c, 0],
+            recv_sem=moving_sem.at[c, 1],
+            device_id=(r, pair_at(4 - 5 * core)),
+            device_id_type=MESH,
         )
 
     for step in range(STEPS):
-        parted[step] = jnp.zeros(parted.shape[1:], jnp.float32)
+        parted[step] = jnp.zeros((width, width), jnp.float32)
+        slot = z * 2 + core
+        squares[step, slot] = jnp.zeros((1, 2 * width + 128), jnp.float32)
 
         @pl.loop(0, CHUNKS)
         def _(c):
@@ -156,29 +190,48 @@
                 sent(step - 1, c).wait_recv()
             left = data[step, 0, chunk_rows(c)]
             right = data[step, 1, chunk_rows(c)]
-            product = dot(split(left), split(right), (0, 0))
-            parted[step, 0, :half] += product[:half]
-            parted[step, 1, :half] += product[half:]
-            parted[step, 0, half : half + 1] += jnp.sum(left * left, axis=0, keepdims=True)
-            parted[step, 0, half + 1 : half + 2] += jnp.sum(right * right, axis=0, keepdims=True)
-
-        choice = plan[step, 0].astype(jnp.float32) * (1 - core).astype(jnp.float32)
-        parted[step, 0, half + 2 : half + 3] = jnp.full((1, width), 1.0, jnp.float32) * choice
-        parted[step, 1, half:] = parted[step, 0, half:]
+            parted[step] += dot(split(left), split(right), (0, 0))
+            squares[step, slot, :, :width] += jnp.sum(left * left, axis=0, keepdims=True)
+            squares[step, slot, :, width : 2 * width] += jnp.sum(
+                right * right, axis=0, keepdims=True
+            )
+
+        choice = plan[step : step + 1, :].astype(jnp.float32) * (1 - core).astype(jnp.float32)
+        squares[step, slot, :, 2 * width :] = jnp.broadcast_to(choice, (1, 128))
 
         if step == 0:
             pl.semaphore_wait(barrier, len(peers))
 
-        partner = (z * 2 + 1 - core, pair_at(step * (2 * core - 1)))
-        exchange = remote(
-            parted.at[step, 1 - core], partner_part.at[step], pair_sem.at[step], partner
-        )
-        exchange.start()
-        exchange.wait_recv()
-        for k in range(4):
-            at = slice(k * quarter, (k + 1) * quarter)
-            shares[step, k, :quarter] = parted[step, core, at] + partner_part[step, at]
-            shares[step, k, quarter:] = parted[step, core, half:] + partner_part[step, half:]
+        partner_pair = pair_at(step * (2 * core - 1))
+        partner = (z * 2 + 1 - core, partner_pair)
+
+        def exchange(j):
+            k = lax.rem(z + j, 4)
+            return remote(
+                parted.at[step, row_at(1 - core, k)],
+                partner_part.at[step, k],
+                pair_sem.at[step, j],
+                partner,
+            )
+
+        def square(j):
+            other = lax.rem(slot + j, 8)
+            same = lax.rem(other, 2) == core
+            return remote(
+                squares.at[step, slot],
+                squares.at[step, slot],
+                square_sem.at[step, j],
+                (other, jnp.where(same, p, partner_pair)),
+            )
+
+        def square_in(j):
+            at = squares.at[step, lax.rem(slot + 8 - j, 8)]
+            return remote(at, at, square_sem.at[step, j], partner)
+
+        for j in (2, 1, 3, 0):
+            exchange(j).start()
+        for j in range(1, 8):
+            square(j).start()
 
         def share(j):
             k = lax.rem(z + j, 4)
@@ -194,14 +247,21 @@
                 (r, pair_at(1)),
             )
 
-        for j in (2, 1, 3):
-            share(j).start()
-        arrived[step, z] = shares[step, z]
+        for j in (2, 1, 3, 0):
+            k = lax.rem(z + j, 4)
+            exchange(j).wait_recv()
+            own = parted[step, row_at(core, k)] + partner_part[step, k]
+            if j:
+                shares[step, k] = own
+                share(j).start()
+            else:
+                arrived[step, k] = own
         for j in (1, 3, 2):
             share_in(j).wait_recv()
-        total = (arrived[step, 0] + arrived[step, 1]) + (arrived[step, 2] + arrived[step, 3])
         mine = row_at(core, z)
-        cross[step, mine] = total[:quarter]
+        cross[step, mine] = (arrived[step, 0] + arrived[step, 1]) + (
+            arrived[step, 2] + arrived[step, 3]
+        )
 
         def gather(j):
             return remote(
@@ -232,9 +292,13 @@
             gather_in(j).wait_recv()
             passed(j).start()
 
-        squares = total[quarter:]
-        left_scale = lax.rsqrt(squares[0:1] + EPSILON)
-        right_scale = lax.rsqrt(squares[1:2] + EPSILON)
+        for j in range(1, 8):
+            square_in(j).wait_recv()
+        total = squares[step, 0]
+        for k in range(1, 8):
+            total = total + squares[step, k]
+        left_scale = lax.rsqrt(total[:, :width] + EPSILON)
+        right_scale = lax.rsqrt(total[:, width : 2 * width] + EPSILON)
         left_scale = jnp.broadcast_to(left_scale, (width, width)).T
         for j in range(4):
             passed_in(j).wait_recv()
@@ -246,8 +310,8 @@
         lower = polynomial(dot(e, e, (0, 0)), eye, g)
         mixed = dot(split(upper), e)
         turned = -mixed.T
-        chosen = squares[2:3] * 0.25
-        flip = core.astype(jnp.float32)
+        chosen = jnp.concatenate([total[:, 2 * width :]] * (width // 128), axis=1) * 0.25
+        flip = core.astype(jnp.float32) if step < STEPS - 1 else 0.0
         second_sent = (chosen * (1.0 - flip) + (1.0 - chosen) * flip) > 0.5
         for at, zero, one in (
             (slice(0, width), upper, mixed),
@@ -271,45 +335,67 @@
             at = chunk_rows(c)
             high, low = split(jnp.concatenate([data[step, 0, at], data[step, 1, at]], axis=1))
             result = dot((high, low), (weights_high[...], weights_low[...]))
-            staged[0, at] = result[:, width:]
             if step < STEPS - 1:
+                staged[0, at] = result[:, width:]
                 sent(step, c).start()
                 data[step + 1, core, at] = result[:, :width]
             else:
-                last_first(c).start()
-                staged[1, at] = result[:, :width]
+                staged[1, at] = result[:, width:]
+
+                @pl.when(detours)
+                def _():
+                    moving_detour(c).start()
+
+                @pl.when(jnp.logical_not(detours))
+                def _():
+                    moving_direct(c).start()
+
+                staged[0, at] = result[:, :width]
 
                 @pl.when(core == 0)
                 def _():
-                    last_local(c).start()
+                    staying_local(c).start()
 
                 @pl.when(core == 1)
                 def _():
-                    last_second(c).start()
-
-        exchange.wait_send()
+                    staying_back(c).start()
+
+        for j in range(4):
+            exchange(j).wait_send()
+            passed(j).wait_send()
         for j in (1, 2, 3):
             share(j).wait_send()
             gather(j).wait_send()
-        for j in range(4):
-            passed(j).wait_send()
+        for j in range(1, 8):
+            square(j).wait_send()
+
+    @pl.when(relays)
+    def _():
+        @pl.loop(0, CHUNKS)
+        def _(c):
+            moving_detour(c).wait_recv()
+            relay(c).start()
 
     @pl.loop(0, CHUNKS)
     def _(c):
-        last_first(c).wait()
+        moving_direct(c).wait()
+
+        @pl.when(relays)
+        def _():
+            relay(c).wait_send()
 
         @pl.when(core == 0)
         def _():
-            last_local(c).wait()
+            staying_local(c).wait()
 
         @pl.when(core == 1)
         def _():
-            last_second(c).wait()
+            staying_back(c).wait()
 
 
 def body(snapshot, plan):
     rows, width = snapshot.shape[0], snapshot.shape[1] // 2
-    half, quarter = width // 2, width // 8
+    quarter = width // 8
     dma = pltpu.SemaphoreType.DMA
     f32 = jnp.float32
     return pl.pallas_call(
@@ -317,29 +403,34 @@
         out_shape=jax.ShapeDtypeStruct(snapshot.shape, f32),
         in_specs=[
             pl.BlockSpec(memory_space=pl.ANY),
-            pl.BlockSpec(memory_space=pltpu.SMEM),
+            pl.BlockSpec(memory_space=pltpu.VMEM),
         ],
         out_specs=pl.BlockSpec(memory_space=pl.ANY),
         scratch_shapes=[
             pltpu.VMEM((STEPS, 2, rows, width), f32),
             pltpu.VMEM((2, rows, width), f32),
-            pltpu.VMEM((STEPS, 2, half + 8, width), f32),
-            pltpu.VMEM((STEPS, half + 8, width), f32),
-            pltpu.VMEM((STEPS, 4, quarter + 8, width), f32),
-            pltpu.VMEM((STEPS, 4, quarter + 8, width), f32),
+            pltpu.VMEM((rows, width), f32),
+            pltpu.VMEM((STEPS, 8, 1, 2 * width + 128), f32),
+            pltpu.VMEM((STEPS, width, width), f32),
+            pltpu.VMEM((STEPS, 4, quarter, width), f32),
+            pltpu.VMEM((STEPS, 4, quarter, width), f32),
+            pltpu.VMEM((STEPS, 4, quarter, width), f32),
             pltpu.VMEM((STEPS, width, width), f32),
             pltpu.VMEM((2 * width, 2 * width), jnp.bfloat16),
             pltpu.VMEM((2 * width, 2 * width), jnp.bfloat16),
             dma((CHUNKS, 2)),
-            dma((STEPS, 2)),
+            dma((STEPS, 8, 2)),
+            dma((STEPS, 4, 2)),
             dma((STEPS, 4, 2)),
             dma((STEPS, 4, 2)),
             dma((STEPS, 4, 2)),
             dma((STEPS, CHUNKS, 2)),
             dma((CHUNKS, 2)),
+            dma((CHUNKS, 2)),
+            dma((CHUNKS, 2)),
         ],
         compiler_params=pltpu.CompilerParams(
-            collective_id=0, has_side_effects=True, vmem_limit_bytes=44 * 1024 * 1024
+            collective_id=0, has_side_effects=True, vmem_limit_bytes=60 * 1024 * 1024
         ),
     )(snapshot, plan)
 

time: 219 us -> 184 us (0.84); the launches traced: 219 us -> 182 us
  Pallas kernels: 214 us -> 176 us
    pallas_call x1, Pallas kernels: 214 us -> 176 us  [body(): pl.pallas_call(functools.partial(kernel, lax.axis_size('pairs')), out_sha...]
    unnamed x4 -> x2, local copies, waits for them, and re-layouts: 4.94 us -> 5.95 us
where the time goes in v2:
time: 184 us; the launch traced here: 182 us
  Pallas kernels  176 us (96%)
  local copies, waits for them, and re-layouts  5.95 us (3%)
    pallas_call x1, Pallas kernels, body(): pl.pallas_call(functools.partial(kernel, lax.axis_size('pairs')), out_sha...  176 us
    unnamed x2, local copies, waits for them, and re-layouts  5.95 us

profile of v2, /device:TPU:5, one launch (start us, length us, event | category | flops | bytes accessed | tf_op | source)
XLA Modules:
  0.0 181.9 jit_solution(7999486614360763646)
XLA Ops:
  0.0 1.3 copy.3.plan
  1.3 175.9 %shard_map.28 = f32[2048,512]{1,0:T(8,128)} custom-call(f32[2048,512]{1,0:T(8,128)} %snapshot.1, s32[3,1]{1,0:T(4,128)} %copy.3.plan), custom_call_target="tpu_custom_call" | custom-call | tf_op jit(solution)/shard_map/pallas_call | solution.py:401
  177.2 4.6 %copy.5 = f32[2048,512]{1,0:T(8,128)} copy(f32[2048,512]{1,0:T(8,128)} %shard_map.28) | data formatting | bytes 8388608

commit v3 on v2

--- a/solution.py
+++ b/solution.py
@@ -228,7 +228,24 @@
             at = squares.at[step, lax.rem(slot + 8 - j, 8)]
             return remote(at, at, square_sem.at[step, j], partner)
 
-        for j in (2, 1, 3, 0):
+        far = lax.rem(z + 2, 4)
+
+        def far_share(t):
+            to = core if t == 0 else 1 - core
+            return remote(
+                parted.at[step, row_at(to, far)],
+                arrived.at[step, z if t == 0 else 4],
+                share_sem.at[step, 2 * t],
+                (far * 2 + to, p if t == 0 else partner_pair),
+            )
+
+        def far_share_in(t):
+            at = arrived.at[step, far if t == 0 else 4]
+            return remote(at, at, share_sem.at[step, 2 * t], partner)
+
+        far_share(0).start()
+        far_share(1).start()
+        for j in (1, 3, 0):
             exchange(j).start()
         for j in range(1, 8):
             square(j).start()
@@ -236,31 +253,29 @@
         def share(j):
             k = lax.rem(z + j, 4)
             return remote(
-                shares.at[step, k], arrived.at[step, z], share_sem.at[step, j], (k * 2 + core, p)
+                shares.at[step, j], arrived.at[step, z], share_sem.at[step, j], (k * 2 + core, p)
             )
 
         def share_in(j):
-            return remote(
-                shares.at[step, z],
-                arrived.at[step, lax.rem(z + 4 - j, 4)],
-                share_sem.at[step, j],
-                (r, pair_at(1)),
-            )
-
-        for j in (2, 1, 3, 0):
+            at = arrived.at[step, lax.rem(z + 4 - j, 4)]
+            return remote(at, at, share_sem.at[step, j], partner)
+
+        for j in (1, 3, 0):
             k = lax.rem(z + j, 4)
             exchange(j).wait_recv()
             own = parted[step, row_at(core, k)] + partner_part[step, k]
             if j:
-                shares[step, k] = own
+                shares[step, j] = own
                 share(j).start()
             else:
                 arrived[step, k] = own
-        for j in (1, 3, 2):
+        for j in (1, 3):
             share_in(j).wait_recv()
+        far_share_in(0).wait_recv()
+        far_share_in(1).wait_recv()
         mine = row_at(core, z)
         cross[step, mine] = (arrived[step, 0] + arrived[step, 1]) + (
-            arrived[step, 2] + arrived[step, 3]
+            (arrived[step, 2] + arrived[step, 3]) + arrived[step, 4]
         )
 
         def gather(j):
@@ -278,8 +293,9 @@
             )
 
         def passed(j):
-            at = row_at(core, lax.rem(z + 4 - j, 4))
-            return remote(cross.at[step, at], cross.at[step, at], pass_sem.at[step, j], partner)
+            at = row_at(core, lax.rem(z + 4 - j, 4) if j != 2 else z)
+            to = partner if j != 2 else (far * 2 + 1 - core, partner_pair)
+            return remote(cross.at[step, at], cross.at[step, at], pass_sem.at[step, j], to)
 
         def passed_in(j):
             at = row_at(1 - core, lax.rem(z + 4 - j, 4))
@@ -287,10 +303,13 @@
 
         for j in (2, 1, 3):
             gather(j).start()
+            if j == 2:
+                passed(2).start()
         passed(0).start()
-        for j in (1, 3, 2):
+        for j in (1, 3):
             gather_in(j).wait_recv()
             passed(j).start()
+        gather_in(2).wait_recv()
 
         for j in range(1, 8):
             square_in(j).wait_recv()
@@ -360,11 +379,15 @@
                 def _():
                     staying_back(c).start()
 
+        far_share(0).wait_send()
+        far_share(1).wait_send()
+        for j in (1, 3, 0):
+            exchange(j).wait_send()
+        for j in (1, 3):
+            share(j).wait_send()
         for j in range(4):
-            exchange(j).wait_send()
             passed(j).wait_send()
         for j in (1, 2, 3):
-            share(j).wait_send()
             gather(j).wait_send()
         for j in range(1, 8):
             square(j).wait_send()
@@ -402,7 +425,7 @@
         functools.partial(kernel, lax.axis_size("pairs")),
         out_shape=jax.ShapeDtypeStruct(snapshot.shape, f32),
         in_specs=[
-            pl.BlockSpec(memory_space=pl.ANY),
+            pl.BlockSpec(memory_space=pltpu.HBM),
             pl.BlockSpec(memory_space=pltpu.VMEM),
         ],
         out_specs=pl.BlockSpec(memory_space=pl.ANY),
@@ -414,7 +437,7 @@
             pltpu.VMEM((STEPS, width, width), f32),
             pltpu.VMEM((STEPS, 4, quarter, width), f32),
             pltpu.VMEM((STEPS, 4, quarter, width), f32),
-            pltpu.VMEM((STEPS, 4, quarter, width), f32),
+            pltpu.VMEM((STEPS, 5, quarter, width), f32),
             pltpu.VMEM((STEPS, width, width), f32),
             pltpu.VMEM((2 * width, 2 * width), jnp.bfloat16),
             pltpu.VMEM((2 * width, 2 * width), jnp.bfloat16),
@@ -430,7 +453,7 @@
             dma((CHUNKS, 2)),
         ],
         compiler_params=pltpu.CompilerParams(
-            collective_id=0, has_side_effects=True, vmem_limit_bytes=60 * 1024 * 1024
+            collective_id=0, has_side_effects=True, vmem_limit_bytes=47 * 1024 * 1024
         ),
     )(snapshot, plan)
 

time: 184 us -> 184 us (level)
  local copies, waits for them, and re-layouts: 5.95 us -> 2.76 us
  Pallas kernels: 176 us -> 179 us
    unnamed x2, local copies, waits for them, and re-layouts: 5.95 us -> 2.76 us
    pallas_call x1, Pallas kernels: 176 us -> 179 us  [body(): pl.pallas_call(functools.partial(kernel, lax.axis_size('pairs')), out_sha...]
where the time goes in v3:
time: 184 us; the launch traced here: 181 us
  Pallas kernels  179 us (97%)
  local copies, waits for them, and re-layouts  2.76 us (2%)
    pallas_call x1, Pallas kernels, body(): pl.pallas_call(functools.partial(kernel, lax.axis_size('pairs')), out_sha...  179 us

profile of v3, /device:TPU:5, one launch (start us, length us, event | category | flops | bytes accessed | tf_op | source)
XLA Modules:
  0.0 181.4 jit_solution(14029547319730595510)
XLA Ops:
  0.0 0.7 copy.3.plan
  0.7 178.7 %shard_map.28 = f32[2048,512]{1,0:T(8,128)S(1)} custom-call(f32[2048,512]{1,0:T(8,128)} %snapshot.1, s32[3,1]{1,0:T(4,128)S(1)} %copy.3.plan), custom_call_target="tpu_custom_call" | custom-call | tf_op jit(solution)/shard_map/pallas_call | solution.py:424
  179.4 2.0 %copy.5 = f32[2048,512]{1,0:T(8,128)} copy(f32[2048,512]{1,0:T(8,128)S(1)} %shard_map.28) | data formatting | bytes 8388608

commit v4 on v3

--- a/solution.py
+++ b/solution.py
@@ -10,6 +10,8 @@
 
 STEPS = 3
 CHUNKS = 8
+DIRECT = (1, 2)
+LAG = 2
 LINE = 4
 EPSILON = 1e-06
 MESH = pl.DeviceIdType.MESH
@@ -190,13 +192,19 @@
                 sent(step - 1, c).wait_recv()
             left = data[step, 0, chunk_rows(c)]
             right = data[step, 1, chunk_rows(c)]
-            parted[step] += dot(split(left), split(right), (0, 0))
+            (left_high, left_low), (right_high, right_low) = split(left), split(right)
+            parted[step] += lax.dot_general(
+                jnp.concatenate([left_high, left_high, left_low], axis=0),
+                jnp.concatenate([right_high, right_low, right_high], axis=0),
+                (((0,), (0,)), ((), ())),
+                preferred_element_type=jnp.float32,
+            )
             squares[step, slot, :, :width] += jnp.sum(left * left, axis=0, keepdims=True)
             squares[step, slot, :, width : 2 * width] += jnp.sum(
                 right * right, axis=0, keepdims=True
             )
 
-        choice = plan[step : step + 1, :].astype(jnp.float32) * (1 - core).astype(jnp.float32)
+        choice = plan[:, step : step + 1].astype(jnp.float32) * (1 - core).astype(jnp.float32)
         squares[step, slot, :, 2 * width :] = jnp.broadcast_to(choice, (1, 128))
 
         if step == 0:
@@ -293,8 +301,9 @@
             )
 
         def passed(j):
-            at = row_at(core, lax.rem(z + 4 - j, 4) if j != 2 else z)
-            to = partner if j != 2 else (far * 2 + 1 - core, partner_pair)
+            direct = j == 2 or step in DIRECT
+            at = row_at(core, z if direct else lax.rem(z + 4 - j, 4))
+            to = (lax.rem(z + j, 4) * 2 + 1 - core, partner_pair) if direct else partner
             return remote(cross.at[step, at], cross.at[step, at], pass_sem.at[step, j], to)
 
         def passed_in(j):
@@ -303,12 +312,13 @@
 
         for j in (2, 1, 3):
             gather(j).start()
-            if j == 2:
-                passed(2).start()
+            if j == 2 or step in DIRECT:
+                passed(j).start()
         passed(0).start()
         for j in (1, 3):
             gather_in(j).wait_recv()
-            passed(j).start()
+            if step not in DIRECT:
+                passed(j).start()
         gather_in(2).wait_recv()
 
         for j in range(1, 8):
@@ -379,6 +389,11 @@
                 def _():
                     staying_back(c).start()
 
+                @pl.when(jnp.logical_and(relays, c >= LAG))
+                def _():
+                    moving_detour(c - LAG).wait_recv()
+                    relay(c - LAG).start()
+
         far_share(0).wait_send()
         far_share(1).wait_send()
         for j in (1, 3, 0):
@@ -394,7 +409,7 @@
 
     @pl.when(relays)
     def _():
-        @pl.loop(0, CHUNKS)
+        @pl.loop(CHUNKS - LAG, CHUNKS)
         def _(c):
             moving_detour(c).wait_recv()
             relay(c).start()
@@ -455,7 +470,7 @@
         compiler_params=pltpu.CompilerParams(
             collective_id=0, has_side_effects=True, vmem_limit_bytes=47 * 1024 * 1024
         ),
-    )(snapshot, plan)
+    )(snapshot, plan.T)
 
 
 def solution(mesh):

time: 184 us -> 178 us (0.967); the launches traced: 181 us -> 177 us
  Pallas kernels: 179 us -> 175 us
    pallas_call x1, Pallas kernels: 179 us -> 175 us  [body(): pl.pallas_call(functools.partial(kernel, lax.axis_size('pairs')), out_sha...]
where the time goes in v4:
time: 178 us; the launch traced here: 177 us
  Pallas kernels  175 us (98%)
  local copies, waits for them, and re-layouts  2.67 us (2%)
    pallas_call x1, Pallas kernels, body(): pl.pallas_call(functools.partial(kernel, lax.axis_size('pairs')), out_sha...  175 us

profile of v4, /device:TPU:5, one launch (start us, length us, event | category | flops | bytes accessed | tf_op | source)
XLA Modules:
  0.0 177.5 jit_solution(12373778937767731277)
XLA Ops:
  0.0 0.0 copy-start
  0.0 0.7 copy-done
  0.7 174.8 %shard_map.28 = f32[2048,512]{1,0:T(8,128)S(1)} custom-call(f32[2048,512]{1,0:T(8,128)} %snapshot.1, s32[1,3]{1,0:T(1,128)S(1)} %bitcast.1), custom_call_target="tpu_custom_call" | custom-call | tf_op jit(solution)/shard_map/pallas_call | solution.py:439
  175.5 2.0 %copy.4 = f32[2048,512]{1,0:T(8,128)} copy(f32[2048,512]{1,0:T(8,128)S(1)} %shard_map.28) | data formatting | bytes 8388608
Async XLA Ops:
  0.0 0.7 copy-start

commit v5 on v4

--- a/solution.py
+++ b/solution.py
@@ -10,6 +10,9 @@
 
 STEPS = 3
 CHUNKS = 8
+RAW = (1, 2, 0)
+PIECES = 4
+PACE = (1, 2, 2, 3)
 DIRECT = (1, 2)
 LAG = 2
 LINE = 4
@@ -36,6 +39,14 @@
         )
 
     return one(a[0], b[0]) + (one(a[0], b[1]) + one(a[1], b[0]))
+
+
+def turn(scaled, eye, g):
+    e = split(scaled)
+    upper = polynomial(dot(e, e, (1, 1)), eye, g)
+    lower = polynomial(dot(e, e, (0, 0)), eye, g)
+    mixed = dot(split(upper), e)
+    return (upper, -mixed.T), (mixed, lower)
 
 
 def polynomial(square, eye, g):
@@ -54,6 +65,9 @@
     data,
     staged,
     relayed,
+    raw,
+    turned_out,
+    turned_in,
     squares,
     parted,
     partner_part,
@@ -72,6 +86,8 @@
     staying_sem,
     moving_sem,
     relay_sem,
+    raw_sem,
+    turned_sem,
 ):
     rows, width = snapshot.shape[0], snapshot.shape[1] // 2
     chunk, half, quarter = rows // CHUNKS, width // 2, width // 8
@@ -125,6 +141,32 @@
         == lax.broadcasted_iota(jnp.int32, (width, width), 1)
     ).astype(jnp.float32)
 
+    piece = chunk // PIECES
+
+    def raw_sent(step, i):
+        start = (CHUNKS - RAW[step]) * chunk + i * piece
+        return remote(
+            data.at[step, :, pl.ds(start, piece)],
+            raw.at[step, :, pl.ds(i * piece, piece)],
+            raw_sem.at[step, i],
+            (r, pair_at(1 - 2 * core)),
+        )
+
+    def start_raw(step, stage):
+        total = RAW[step] * PIECES
+        low = min(sum(PACE[:stage]), total)
+        high = total if stage == 3 else min(sum(PACE[: stage + 1]), total)
+        for i in range(low, high):
+            raw_sent(step, i).start()
+
+    def turned(step):
+        return remote(
+            turned_out.at[step],
+            turned_in.at[step],
+            turned_sem.at[step],
+            (r, pair_at(1 - 2 * core)),
+        )
+
     def sent(step, c):
         return remote(
             staged.at[0, chunk_rows(c)],
@@ -183,13 +225,7 @@
         slot = z * 2 + core
         squares[step, slot] = jnp.zeros((1, 2 * width + 128), jnp.float32)
 
-        @pl.loop(0, CHUNKS)
-        def _(c):
-            if step == 0:
-                load(c, 0).wait()
-                load(c, 1).wait()
-            else:
-                sent(step - 1, c).wait_recv()
+        def gram(c):
             left = data[step, 0, chunk_rows(c)]
             right = data[step, 1, chunk_rows(c)]
             (left_high, left_low), (right_high, right_low) = split(left), split(right)
@@ -204,6 +240,21 @@
                 right * right, axis=0, keepdims=True
             )
 
+        if step == 0:
+
+            @pl.loop(0, CHUNKS)
+            def _(c):
+                load(c, 0).wait()
+                load(c, 1).wait()
+                gram(c)
+        else:
+            pl.loop(CHUNKS - RAW[step - 1], CHUNKS)(gram)
+
+            @pl.loop(0, CHUNKS - RAW[step - 1])
+            def _(c):
+                sent(step - 1, c).wait_recv()
+                gram(c)
+
         choice = plan[:, step : step + 1].astype(jnp.float32) * (1 - core).astype(jnp.float32)
         squares[step, slot, :, 2 * width :] = jnp.broadcast_to(choice, (1, 128))
 
@@ -257,6 +308,7 @@
             exchange(j).start()
         for j in range(1, 8):
             square(j).start()
+        start_raw(step, 0)
 
         def share(j):
             k = lax.rem(z + j, 4)
@@ -277,6 +329,7 @@
                 share(j).start()
             else:
                 arrived[step, k] = own
+        start_raw(step, 1)
         for j in (1, 3):
             share_in(j).wait_recv()
         far_share_in(0).wait_recv()
@@ -315,10 +368,12 @@
             if j == 2 or step in DIRECT:
                 passed(j).start()
         passed(0).start()
+        start_raw(step, 2)
         for j in (1, 3):
             gather_in(j).wait_recv()
             if step not in DIRECT:
                 passed(j).start()
+        start_raw(step, 3)
         gather_in(2).wait_recv()
 
         for j in range(1, 8):
@@ -334,28 +389,26 @@
 
         scaled = 0.5 * cross[step] * left_scale * right_scale
         scaled = scaled / (1.0 + jnp.sqrt(jnp.sum(scaled * scaled)))
-        e = split(scaled)
-        upper = polynomial(dot(e, e, (1, 1)), eye, g)
-        lower = polynomial(dot(e, e, (0, 0)), eye, g)
-        mixed = dot(split(upper), e)
-        turned = -mixed.T
         chosen = jnp.concatenate([total[:, 2 * width :]] * (width // 128), axis=1) * 0.25
         flip = core.astype(jnp.float32) if step < STEPS - 1 else 0.0
-        second_sent = (chosen * (1.0 - flip) + (1.0 - chosen) * flip) > 0.5
-        for at, zero, one in (
-            (slice(0, width), upper, mixed),
-            (slice(width, 2 * width), turned, lower),
-        ):
-            kept_high, kept_low = split(jnp.where(second_sent, zero, one))
-            sent_high, sent_low = split(jnp.where(second_sent, one, zero))
-            weights_high[at, :width] = kept_high
-            weights_high[at, width:] = sent_high
-            weights_low[at, :width] = kept_low
-            weights_low[at, width:] = sent_low
+        second_sent = chosen * (1.0 - flip) + (1.0 - chosen) * flip
+        if step < STEPS - 1:
+            turned_out[step, :width] = scaled
+            turned_out[step, width:] = jnp.broadcast_to(second_sent, (8, width))
+            turned(step).start()
+        zero, one = turn(scaled, eye, g)
+
+        def put(side, pick, zero, one):
+            for k in range(2):
+                at = slice(k * width, (k + 1) * width), slice(side * width, (side + 1) * width)
+                weights_high[at], weights_low[at] = split(jnp.where(pick > 0.5, one[k], zero[k]))
+
+        put(0, 1.0 - second_sent, zero, one)
+        put(1, second_sent, zero, one)
 
         if step > 0:
 
-            @pl.loop(0, CHUNKS)
+            @pl.loop(0, CHUNKS - RAW[step - 1])
             def _(c):
                 sent(step - 1, c).wait_send()
 
@@ -366,8 +419,11 @@
             result = dot((high, low), (weights_high[...], weights_low[...]))
             if step < STEPS - 1:
                 staged[0, at] = result[:, width:]
-                sent(step, c).start()
                 data[step + 1, core, at] = result[:, :width]
+
+                @pl.when(c < CHUNKS - RAW[step])
+                def _():
+                    sent(step, c).start()
             else:
                 staged[1, at] = result[:, width:]
 
@@ -393,6 +449,25 @@
                 def _():
                     moving_detour(c - LAG).wait_recv()
                     relay(c - LAG).start()
+
+        if step < STEPS - 1:
+            turned(step).wait_recv()
+            zero, one = turn(turned_in[step, :width], eye, g)
+            put(1, turned_in[step, width : width + 1], zero, one)
+            for i in range(RAW[step] * PIECES):
+                raw_sent(step, i).wait_recv()
+
+            @pl.loop(0, RAW[step])
+            def _(i):
+                at = chunk_rows(i)
+                high, low = split(jnp.concatenate([raw[step, 0, at], raw[step, 1, at]], axis=1))
+                data[step + 1, 1 - core, chunk_rows(i + CHUNKS - RAW[step])] = dot(
+                    (high, low), (weights_high[:, width:], weights_low[:, width:])
+                )
+
+            turned(step).wait_send()
+            for i in range(RAW[step] * PIECES):
+                raw_sent(step, i).wait_send()
 
         far_share(0).wait_send()
         far_share(1).wait_send()
@@ -448,6 +523,9 @@
             pltpu.VMEM((STEPS, 2, rows, width), f32),
             pltpu.VMEM((2, rows, width), f32),
             pltpu.VMEM((rows, width), f32),
+            pltpu.VMEM((STEPS - 1, 2, max(RAW) * rows // CHUNKS, width), f32),
+            pltpu.VMEM((STEPS - 1, width + 8, width), f32),
+            pltpu.VMEM((STEPS - 1, width + 8, width), f32),
             pltpu.VMEM((STEPS, 8, 1, 2 * width + 128), f32),
             pltpu.VMEM((STEPS, width, width), f32),
             pltpu.VMEM((STEPS, 4, quarter, width), f32),
@@ -466,6 +544,8 @@
             dma((CHUNKS, 2)),
             dma((CHUNKS, 2)),
             dma((CHUNKS, 2)),
+            dma((STEPS, max(RAW) * PIECES, 2)),
+            dma((STEPS, 2)),
         ],
         compiler_params=pltpu.CompilerParams(
             collective_id=0, has_side_effects=True, vmem_limit_bytes=47 * 1024 * 1024

time: 178 us -> 179 us (level); the launches traced: 177 us -> 176 us
  Pallas kernels: 175 us -> 173 us
where the time goes in v5:
time: 179 us; the launch traced here: 176 us
  Pallas kernels  173 us (97%)
  local copies, waits for them, and re-layouts  2.67 us (1%)
    pallas_call x1, Pallas kernels, body(): pl.pallas_call(functools.partial(kernel, lax.axis_size('pairs')), out_sha...  173 us

profile of v5, /device:TPU:5, one launch (start us, length us, event | category | flops | bytes accessed | tf_op | source)
XLA Modules:
  0.0 175.7 jit_solution(5476037464182354538)
XLA Ops:
  0.0 0.0 copy-start
  0.0 0.7 copy-done
  0.7 173.1 %shard_map.28 = f32[2048,512]{1,0:T(8,128)S(1)} custom-call(f32[2048,512]{1,0:T(8,128)} %snapshot.1, s32[1,3]{1,0:T(1,128)S(1)} %bitcast.1), custom_call_target="tpu_custom_call" | custom-call | tf_op jit(solution)/shard_map/pallas_call | solution.py:514
  173.7 2.0 %copy.4 = f32[2048,512]{1,0:T(8,128)} copy(f32[2048,512]{1,0:T(8,128)S(1)} %shard_map.28) | data formatting | bytes 8388608
Async XLA Ops:
  0.0 0.7 copy-start

commit v6 on v4

--- a/solution.py
+++ b/solution.py
@@ -251,10 +251,28 @@
             at = arrived.at[step, far if t == 0 else 4]
             return remote(at, at, share_sem.at[step, 2 * t], partner)
 
-        far_share(0).start()
-        far_share(1).start()
-        for j in (1, 3, 0):
-            exchange(j).start()
+        def straight(t, j):
+            k, to = lax.rem(z + j, 4), core if t == 0 else 1 - core
+            return remote(
+                parted.at[step, row_at(to, k)],
+                arrived.at[step, z + 4 * t],
+                (share_sem if t == 0 else pair_sem).at[step, j],
+                (k * 2 + to, p if t == 0 else partner_pair),
+            )
+
+        def straight_in(t, j):
+            at = arrived.at[step, lax.rem(z + 4 - j, 4) + 4 * t]
+            return remote(at, at, (share_sem if t == 0 else pair_sem).at[step, j], partner)
+
+        ways = ((0, 2), (1, 2), (0, 1), (0, 3), (1, 1), (1, 3), (1, 0))
+        if step in DIRECT:
+            for t, j in ways:
+                straight(t, j).start()
+        else:
+            far_share(0).start()
+            far_share(1).start()
+            for j in (1, 3, 0):
+                exchange(j).start()
         for j in range(1, 8):
             square(j).start()
 
@@ -268,23 +286,30 @@
             at = arrived.at[step, lax.rem(z + 4 - j, 4)]
             return remote(at, at, share_sem.at[step, j], partner)
 
-        for j in (1, 3, 0):
-            k = lax.rem(z + j, 4)
-            exchange(j).wait_recv()
-            own = parted[step, row_at(core, k)] + partner_part[step, k]
-            if j:
-                shares[step, j] = own
-                share(j).start()
-            else:
-                arrived[step, k] = own
-        for j in (1, 3):
-            share_in(j).wait_recv()
-        far_share_in(0).wait_recv()
-        far_share_in(1).wait_recv()
         mine = row_at(core, z)
-        cross[step, mine] = (arrived[step, 0] + arrived[step, 1]) + (
-            (arrived[step, 2] + arrived[step, 3]) + arrived[step, 4]
-        )
+        if step in DIRECT:
+            total = parted[step, mine]
+            for t, j in ways[::-1]:
+                straight_in(t, j).wait_recv()
+                total = total + arrived[step, lax.rem(z + 4 - j, 4) + 4 * t]
+            cross[step, mine] = total
+        else:
+            for j in (1, 3, 0):
+                k = lax.rem(z + j, 4)
+                exchange(j).wait_recv()
+                own = parted[step, row_at(core, k)] + partner_part[step, k]
+                if j:
+                    shares[step, j] = own
+                    share(j).start()
+                else:
+                    arrived[step, k] = own
+            for j in (1, 3):
+                share_in(j).wait_recv()
+            far_share_in(0).wait_recv()
+            far_share_in(1).wait_recv()
+            cross[step, mine] = (arrived[step, 0] + arrived[step, 1]) + (
+                (arrived[step, 2] + arrived[step, 3]) + arrived[step, 4]
+            )
 
         def gather(j):
             return remote(
@@ -394,12 +419,16 @@
                     moving_detour(c - LAG).wait_recv()
                     relay(c - LAG).start()
 
-        far_share(0).wait_send()
-        far_share(1).wait_send()
-        for j in (1, 3, 0):
-            exchange(j).wait_send()
-        for j in (1, 3):
-            share(j).wait_send()
+        if step in DIRECT:
+            for t, j in ways:
+                straight(t, j).wait_send()
+        else:
+            far_share(0).wait_send()
+            far_share(1).wait_send()
+            for j in (1, 3, 0):
+                exchange(j).wait_send()
+            for j in (1, 3):
+                share(j).wait_send()
         for j in range(4):
             passed(j).wait_send()
         for j in (1, 2, 3):
@@ -452,7 +481,7 @@
             pltpu.VMEM((STEPS, width, width), f32),
             pltpu.VMEM((STEPS, 4, quarter, width), f32),
             pltpu.VMEM((STEPS, 4, quarter, width), f32),
-            pltpu.VMEM((STEPS, 5, quarter, width), f32),
+            pltpu.VMEM((STEPS, 8, quarter, width), f32),
             pltpu.VMEM((STEPS, width, width), f32),
             pltpu.VMEM((2 * width, 2 * width), jnp.bfloat16),
             pltpu.VMEM((2 * width, 2 * width), jnp.bfloat16),

time: 178 us -> 177 us (level)
  Pallas kernels: 175 us -> 173 us
    pallas_call x1, Pallas kernels: 175 us -> 173 us  [body(): pl.pallas_call(functools.partial(kernel, lax.axis_size('pairs')), out_sha...]
where the time goes in v6:
time: 177 us; the launch traced here: 175 us
  Pallas kernels  173 us (98%)
  local copies, waits for them, and re-layouts  2.67 us (2%)
    pallas_call x1, Pallas kernels, body(): pl.pallas_call(functools.partial(kernel, lax.axis_size('pairs')), out_sha...  173 us

profile of v6, /device:TPU:5, one launch (start us, length us, event | category | flops | bytes accessed | tf_op | source)
XLA Modules:
  0.0 175.3 jit_solution(14592843301197822074)
XLA Ops:
  0.0 0.0 copy-start
  0.0 0.7 copy-done
  0.7 172.6 %shard_map.28 = f32[2048,512]{1,0:T(8,128)S(1)} custom-call(f32[2048,512]{1,0:T(8,128)} %snapshot.1, s32[1,3]{1,0:T(1,128)S(1)} %bitcast.1), custom_call_target="tpu_custom_call" | custom-call | tf_op jit(solution)/shard_map/pallas_call | solution.py:468
  173.3 2.0 %copy.4 = f32[2048,512]{1,0:T(8,128)} copy(f32[2048,512]{1,0:T(8,128)S(1)} %shard_map.28) | data formatting | bytes 8388608
Async XLA Ops:
  0.0 0.7 copy-start

commit v7 on v6

--- a/solution.py
+++ b/solution.py
@@ -11,7 +11,7 @@
 STEPS = 3
 CHUNKS = 8
 DIRECT = (1, 2)
-LAG = 2
+LAG = 3
 LINE = 4
 EPSILON = 1e-06
 MESH = pl.DeviceIdType.MESH

time: 177 us -> 177 us (level)
  no operation moved by 1% of the time
where the time goes in v7:
time: 177 us; the launch traced here: 175 us
  Pallas kernels  173 us (98%)
  local copies, waits for them, and re-layouts  2.67 us (2%)
    pallas_call x1, Pallas kernels, body(): pl.pallas_call(functools.partial(kernel, lax.axis_size('pairs')), out_sha...  173 us

profile of v7, /device:TPU:5, one launch (start us, length us, event | category | flops | bytes accessed | tf_op | source)
XLA Modules:
  0.0 175.3 jit_solution(6626561887806182119)
XLA Ops:
  0.0 0.0 copy-start
  0.0 0.7 copy-done
  0.7 172.6 %shard_map.28 = f32[2048,512]{1,0:T(8,128)S(1)} custom-call(f32[2048,512]{1,0:T(8,128)} %snapshot.1, s32[1,3]{1,0:T(1,128)S(1)} %bitcast.1), custom_call_target="tpu_custom_call" | custom-call | tf_op jit(solution)/shard_map/pallas_call | solution.py:468
  173.3 2.0 %copy.4 = f32[2048,512]{1,0:T(8,128)} copy(f32[2048,512]{1,0:T(8,128)S(1)} %shard_map.28) | data formatting | bytes 8388608
Async XLA Ops:
  0.0 0.7 copy-start
